TPU v7x, 512 devices: a whole 4x4x16 slice. The times are simulated.
512 devices in a mesh: wide: 64 (over y_hi, z, core), narrow: 8 (over x, y_lo).
Axes of the slice: x: 4, y: 4 (y_hi: 2, y_lo: 2; y = y_hi * 2 + y_lo), z: 16, core: 2. Of those that a mesh axis runs over, the one named last changes fastest.
Arguments:
- examples: bfloat16 [320, 8192], P('wide', 'narrow'), may hold values from -6 to 6
- references: bfloat16 [128, 8192], P('wide', 'narrow'), may hold values from -6 to 6
- gate_weight: bfloat16 [8192, 28672], P('narrow', 'wide'), may hold values from -0.0625 to 0.0625
- up_weight: bfloat16 [8192, 28672], P('narrow', 'wide'), may hold values from -0.0625 to 0.0625
- down_weight: bfloat16 [28672, 8192], P('wide', 'narrow'), may hold values from -0.03125 to 0.03125
- cotangent: bfloat16 [320, 8192], P('wide', 'narrow'), may hold values from -6 to 6
- pair_ref: int32 [320, 4], replicated, may hold values from 0 to 127
- points: int32 [8], replicated, may hold values from 1 to 8
Outputs:
- expected: bfloat16 [320, 8192], P('wide', 'narrow')
All inputs are finite; a program needn't handle non-finite values.
Results may differ from a plain program's by a relative error of at most 0.005.
Values may be sent and summed in bfloat16 or wider, within the bound.
A program may use at most 64 MiB of HBM per device.

v0:
```python
import jax
import jax.numpy as jnp
from jax import lax
from jax.sharding import Mesh
from jax.sharding import PartitionSpec as P

WIDE = ("wide_0", "wide_1", "wide_2")


def copy_for_each(x, axis):
    size = lax.axis_size(axis)
    return lax.all_to_all(jnp.broadcast_to(x[None], (size, *x.shape)), axis, 0, 0, tiled=True)


def in_order(blocks, dim):
    blocks = jnp.moveaxis(blocks, 0, dim)
    dims = blocks.shape
    return blocks.reshape(*dims[:dim], dims[dim] * dims[dim + 1], *dims[dim + 2 :])


def gather_axes(x, axes, dim):
    far, near = axes
    blocks = copy_for_each(copy_for_each(x, far), near)
    return in_order(blocks.swapaxes(0, 1).reshape(-1, *x.shape), dim)


def cut_along(x, dim, size):
    before, after = (x.shape[:dim], x.shape[dim + 1 :])
    return jnp.moveaxis(x.reshape(*before, size, -1, *after), dim, 0)


def summed_on_arrival(x, axis, dim):
    blocks = cut_along(x, dim, lax.axis_size(axis))
    arrived = lax.all_to_all(blocks, axis, split_axis=0, concat_axis=0, tiled=True)
    return arrived.sum(axis=0)


def sent_together(arrays, axis, dim, along):
    both = jnp.concatenate(arrays, axis=along)
    out, at, outs = (summed_on_arrival(both, axis, dim), 0, [])
    for a in arrays:
        outs.append(lax.slice_in_dim(out, at, at + a.shape[along], axis=along))
        at += a.shape[along]
    return tuple(outs)


def turned_gather(arrays, axis, dims):
    turned = [jnp.moveaxis(a, dim, 0) for a, dim in zip(arrays, dims)]
    widths = [t[0].size for t in turned]
    both = jnp.concatenate([t.reshape(-1, w) for t, w in zip(turned, widths)], axis=1)
    out = lax.all_gather(both, axis, axis=0, tiled=True)
    blocks = jnp.split(out, [sum(widths[:k]) for k in range(1, len(widths))], axis=1)
    return tuple(
        (
            jnp.moveaxis(b.reshape(-1, *t.shape[1:]), 0, dim)
            for b, t, dim in zip(blocks, turned, dims)
        )
    )


def sum_in_two_steps(x, axes, dim):
    far, near = axes
    own = summed_on_arrival(cut_along(x, dim, lax.axis_size(far)), near, dim + 1)
    return jnp.sum(lax.all_to_all(own, far, 0, 0, tiled=True), axis=0)


def path_coefficients(example_gate, example_up, reference_gate, reference_up, pair_ref, points):
    alphas = points.astype(jnp.float32) / 8.0
    coef_gate = jnp.zeros(example_gate.shape, jnp.float32)
    coef_up = jnp.zeros(example_gate.shape, jnp.float32)
    for pair_slot in range(pair_ref.shape[1]):
        chosen = pair_ref[:, pair_slot]
        base_gate = jnp.take(reference_gate, chosen, axis=0)
        base_up = jnp.take(reference_up, chosen, axis=0)
        step_gate = example_gate - base_gate
        step_up = example_up - base_up
        for point_slot in range(alphas.shape[0]):
            position = alphas[point_slot]
            along_gate = base_gate + position * step_gate
            along_up = base_up + position * step_up
            sigmoid = jax.nn.sigmoid(along_gate)
            coef_gate = coef_gate + along_up * sigmoid * (1.0 + along_gate * (1.0 - sigmoid))
            coef_up = coef_up + along_gate * sigmoid
    total = pair_ref.shape[1] * alphas.shape[0]
    return (coef_gate / total, coef_up / total)


def transposed_product(left, right):
    return lax.dot_general(
        left, right, (((1,), (1,)), ((), ())), preferred_element_type=jnp.float32
    )


def on_device(
    examples, references, gate_weight, up_weight, down_weight, cotangent, pair_ref, points
):
    all_examples, all_references, all_cotangent = (
        gather_axes(examples, (("wide_0", "wide_1"), "wide_2"), 0),
        gather_axes(references, (("wide_0", "wide_1"), "wide_2"), 0),
        gather_axes(cotangent, (("wide_0", "wide_1"), "wide_2"), 0),
    )
    gate_terms = jnp.dot(all_examples, gate_weight, preferred_element_type=jnp.float32)
    up_terms = jnp.dot(all_examples, up_weight, preferred_element_type=jnp.float32)
    reference_gate_terms = jnp.dot(all_references, gate_weight, preferred_element_type=jnp.float32)
    reference_up_terms = jnp.dot(all_references, up_weight, preferred_element_type=jnp.float32)
    upstream_terms = transposed_product(all_cotangent, down_weight)
    example_gate, example_up, reference_gate, reference_up, upstream = sent_together(
        (gate_terms, up_terms, reference_gate_terms, reference_up_terms, upstream_terms),
        "narrow",
        1,
        0,
    )
    coef_gate, coef_up = path_coefficients(
        example_gate, example_up, reference_gate, reference_up, pair_ref, points
    )
    grad_gate = (upstream * coef_gate).astype(jnp.bfloat16)
    grad_up = (upstream * coef_up).astype(jnp.bfloat16)
    full_gate, full_up = turned_gather((grad_gate, grad_up), "narrow", (1, 1))
    result = sum_in_two_steps(
        transposed_product(full_gate, gate_weight) + transposed_product(full_up, up_weight),
        (("wide_0", "wide_1"), "wide_2"),
        0,
    )
    return result.astype(jnp.bfloat16)


def solution(mesh):
    split = Mesh(
        mesh.devices.reshape(2, 16, 2, mesh.shape["narrow"]),
        ("wide_0", "wide_1", "wide_2", "narrow"),
    )
    placed = (
        P(WIDE, "narrow"),
        P(WIDE, "narrow"),
        P("narrow", WIDE),
        P("narrow", WIDE),
        P(WIDE, "narrow"),
        P(WIDE, "narrow"),
        P(),
        P(),
    )
    return jax.shard_map(
        on_device, mesh=split, in_specs=placed, out_specs=P(WIDE, "narrow"), check_vma=False
    )
```

profile of v0, /device:TPU:1, one launch (start us, length us, event | category | flops | bytes accessed | tf_op | source)
XLA Modules:
  0.0 291.8 jit_solution(9119121526575013563)
XLA Ops:
  0.8 34.6 %all_to_all.45 = bf16[32,2,1024]{2,1,0:T(2,128)(2,1)S(1)} all-to-all(bf16[32,2,1024]{2,1,0:T(2,128)(2,1)S(1)} %broadcast_in_dim.20), channel_id=1, replica_groups=mesh['wide_0'=2,'wide_1'=16,'wide_2'=2,'narrow'=8] {'wide_0','wide_1'}, dimensions={0} | all-to-all | bytes 262144 | tf_op jit(solution)/shard_map/all_to_all | solution.py:12
  36.2 35.4 %all_to_all.46 = bf16[32,5,1024]{2,1,0:T(8,128)(2,1)S(1)} all-to-all(bf16[32,5,1024]{2,1,0:T(8,128)(2,1)S(1)} %broadcast_in_dim.18), channel_id=1, replica_groups=mesh['wide_0'=2,'wide_1'=16,'wide_2'=2,'narrow'=8] {'wide_0','wide_1'}, dimensions={0} | all-to-all | bytes 655360 | tf_op jit(solution)/shard_map/all_to_all | solution.py:12
  72.4 6.9 %all-to-all-start.3 = ((bf16[2,32,2,1024]{3,2,1,0:T(2,128)(2,1)}), bf16[2,32,2,1024]{3,2,1,0:T(2,128)(2,1)S(1)}, u32[]{:S(2)}, u32[]{:S(2)}) async-start(bf16[2,32,2,1024]{3,2,1,0:T(2,128)(2,1)} %broadcast_in_dim.21), calls=%async_computation.3 | async-start | bytes 524288 | tf_op jit(solution)/shard_map/all_to_all | solution.py:12
  80.6 4.2 %all_to_all.47 = bf16[2,32,5,1024]{3,1,2,0:T(8,128)(2,1)S(1)} all-to-all(bf16[2,32,5,1024]{3,1,2,0:T(8,128)(2,1)S(1)} %broadcast_in_dim.19), channel_id=1, replica_groups=mesh['wide_0'=2,'wide_1'=16,'wide_2'=2,'narrow'=8] {'wide_2'}, dimensions={0} | all-to-all | bytes 1310720 | tf_op jit(solution)/shard_map/all_to_all | solution.py:12
  85.8 4.6 %all-to-all-start.4 = ((bf16[32,5,1024]{2,1,0:T(8,128)(2,1)}), bf16[32,5,1024]{2,1,0:T(8,128)(2,1)}, u32[]{:S(2)}, u32[]{:S(2)}) async-start(bf16[32,5,1024]{2,1,0:T(8,128)(2,1)} %broadcast_in_dim.22), calls=%async_computation.4 | async-start | bytes 1048576 | tf_op jit(solution)/shard_map/all_to_all | solution.py:12
  92.1 1.4 convolution_dynamic-update-slice_fusion.2
  93.4 1.4 convolution_dynamic-update-slice_fusion.1
  94.8 1.2 convolution_dynamic-update-slice_fusion.4
  96.0 1.1 convolution_dynamic-update-slice_fusion.3
  97.1 25.6 %all-to-all-done.4 = bf16[32,5,1024]{2,1,0:T(8,128)(2,1)} async-done(((bf16[32,5,1024]{2,1,0:T(8,128)(2,1)}), bf16[32,5,1024]{2,1,0:T(8,128)(2,1)}, u32[]{:S(2)}, u32[]{:S(2)}) %all-to-all-start.4) | async-done | bytes 327712 | tf_op jit(solution)/shard_map/all_to_all | solution.py:12
  122.7 1.3 copy.64
  124.1 4.9 %all_to_all.48 = bf16[2,32,5,1024]{3,1,2,0:T(8,128)(2,1)S(1)} all-to-all(bf16[2,32,5,1024]{3,1,2,0:T(8,128)(2,1)S(1)} %broadcast_in_dim.23), channel_id=1, replica_groups=mesh['wide_0'=2,'wide_1'=16,'wide_2'=2,'narrow'=8] {'wide_2'}, dimensions={0} | all-to-all | bytes 1310720 | tf_op jit(solution)/shard_map/all_to_all | solution.py:12
  129.6 1.4 convolution_dynamic-update-slice_fusion
  131.0 3.1 %copy.68 = f32[1216,448]{0,1:T(8,128)} copy(f32[1216,448]{1,0:T(8,128)} %convolution_dynamic-update-slice_fusion) | data formatting | bytes 4358144 | tf_op jit(solution)/shard_map/concatenate | solution.py:39
  134.1 4.3 %all-to-all-start.6 = ((f32[8,1216,56]{1,2,0:T(8,128)}), f32[8,1216,56]{1,2,0:T(8,128)S(1)}, u32[]{:S(2)}, u32[]{:S(2)}) async-start(f32[8,1216,56]{1,2,0:T(8,128)} %bitcast.31), calls=%async_computation.6 | async-start | bytes 4587520 | tf_op jit(solution)/shard_map/all_to_all | solution.py:34
  139.2 32.7 %all-to-all-done.6 = f32[8,1216,56]{1,2,0:T(8,128)S(1)} async-done(((f32[8,1216,56]{1,2,0:T(8,128)}), f32[8,1216,56]{1,2,0:T(8,128)S(1)}, u32[]{:S(2)}, u32[]{:S(2)}) %all-to-all-start.6) | async-done | bytes 2179104 | tf_op jit(solution)/shard_map/all_to_all | solution.py:34
  172.2 1.1 gather_fusion.3
  181.9 5.7 %fusion.14 = bf16[56,320]{1,0:T(8,128)(2,1)S(1)} fusion(f32[1216,56]{0,1:T(8,128)S(1)} %reduce_sum.27, f32[]{:T(128)} %bitcast.5, f32[320,56]{0,1:T(8,128)S(1)} %copy.72, pred[320]{0:T(512)(128)(4,1)S(1)} %get-tuple-element.27, f32[]{:T(128)} %bitcast.6, f32[]{:T(128)} %bitcast.7, f32[]{:T(128)} %bitcast.8, f32[]{:T(128)} %bitcast.9, f32[]{:T(128)} %bitcast.10, ...), kind=kLoop, calls=%fused_computation.102 | loop fusion | flops 4193280 | bytes 467232 | tf_op jit(solution)/shard_map/transpose | solution.py:48
  187.7 6.3 %fusion.15 = bf16[56,320]{1,0:T(8,128)(2,1)S(1)} fusion(f32[320,56]{0,1:T(8,128)S(1)} %copy.77, pred[320]{0:T(512)(128)(4,1)S(1)} %get-tuple-element.24, f32[320,56]{0,1:T(8,128)S(1)} %copy.75, pred[320]{0:T(512)(128)(4,1)S(1)} %get-tuple-element.25, f32[320,56]{0,1:T(8,128)S(1)} %copy.73, pred[320]{0:T(512)(128)(4,1)S(1)} %get-tuple-element.26, ...), kind=kLoop, calls=%fused_computation.103 | loop fusion | flops 7777280 | bytes 825632 | tf_op jit(solution)/shard_map/transpose | solution.py:48
  194.1 23.3 %all_gather.3 = bf16[448,640]{1,0:T(8,128)(2,1)S(1)} all-gather(bf16[56,640]{1,0:T(8,128)(2,1)S(1)} %pad_maximum_fusion), channel_id=1, replica_groups=mesh['wide_0'=2,'wide_1'=16,'wide_2'=2,'narrow'=8] {'narrow'}, dimensions={0}, use_global_device_ids=true | all-gather | bytes 645120 | tf_op jit(solution)/shard_map/all_gather | solution.py:51
  218.0 1.8 convolution_add_fusion
  219.7 1.4 reshape_reshape.15
  221.9 11.9 %all_to_all.49 = f32[2,32,5,1024]{3,1,2,0:T(8,128)S(1)} all-to-all(f32[2,32,5,1024]{3,1,2,0:T(8,128)S(1)} %copy.79), channel_id=1, replica_groups=mesh['wide_0'=2,'wide_1'=16,'wide_2'=2,'narrow'=8] {'wide_2'}, dimensions={0} | all-to-all | bytes 2621440 | tf_op jit(solution)/shard_map/all_to_all | solution.py:34
  234.3 56.8 %all_to_all.50 = f32[32,5,1024]{2,1,0:T(8,128)S(1)} all-to-all(f32[32,5,1024]{2,1,0:T(8,128)S(1)} %copy.80), channel_id=1, replica_groups=mesh['wide_0'=2,'wide_1'=16,'wide_2'=2,'narrow'=8] {'wide_0','wide_1'}, dimensions={0} | all-to-all | bytes 1310720 | tf_op jit(solution)/shard_map/all_to_all | solution.py:64
  (66 shorter events, 19.1 us)
Async XLA Ops:
  0.0 92.0 %copy-start = (bf16[1024,448]{0,1:T(8,128)(2,1)S(1)}, bf16[1024,448]{0,1:T(8,128)(2,1)}, u32[]{:S(2)}) copy-start(bf16[1024,448]{0,1:T(8,128)(2,1)} %param.12) | copy-start | bytes 2752516
  36.2 48.7 %copy-start.5 = (bf16[5,1024]{1,0:T(8,128)(2,1)S(1)}, bf16[5,1024]{1,0:T(8,128)(2,1)}, u32[]{:S(2)}) copy-start(bf16[5,1024]{1,0:T(8,128)(2,1)} %param.15) | copy-start | bytes 30724
  72.4 8.1 %all-to-all-start.3 = ((bf16[2,32,2,1024]{3,2,1,0:T(2,128)(2,1)}), bf16[2,32,2,1024]{3,2,1,0:T(2,128)(2,1)S(1)}, u32[]{:S(2)}, u32[]{:S(2)}) async-start(bf16[2,32,2,1024]{3,2,1,0:T(2,128)(2,1)} %broadcast_in_dim.21), calls=%async_computation.3 | async-start | bytes 524288 | tf_op jit(solution)/shard_map/all_to_all | solution.py:12
  85.8 36.9 %all-to-all-start.4 = ((bf16[32,5,1024]{2,1,0:T(8,128)(2,1)}), bf16[32,5,1024]{2,1,0:T(8,128)(2,1)}, u32[]{:S(2)}, u32[]{:S(2)}) async-start(bf16[32,5,1024]{2,1,0:T(8,128)(2,1)} %broadcast_in_dim.22), calls=%async_computation.4 | async-start | bytes 1048576 | tf_op jit(solution)/shard_map/all_to_all | solution.py:12
  91.4 2.1 copy-start.1
  92.0 2.8 copy-start.3
  124.0 5.6 %copy-start.4 = (bf16[448,1024]{1,0:T(8,128)(2,1)S(1)}, bf16[448,1024]{1,0:T(8,128)(2,1)}, u32[]{:S(2)}) copy-start(bf16[448,1024]{1,0:T(8,128)(2,1)} %param.14) | copy-start | bytes 2752516
  134.1 4.3 %copy-start.6 = (s32[320,4]{0,1:T(4,128)S(1)}, s32[320,4]{0,1:T(4,128)}, u32[]{:S(2)}) copy-start(s32[320,4]{0,1:T(4,128)} %param.16) | copy-start | bytes 15364
  134.1 4.4 %copy-start.7 = (s32[8]{0:T(128)S(1)}, s32[8]{0:T(128)}, u32[]{:S(2)}) copy-start(s32[8]{0:T(128)} %param.17) | copy-start | bytes 100
  134.1 37.8 %all-to-all-start.6 = ((f32[8,1216,56]{1,2,0:T(8,128)}), f32[8,1216,56]{1,2,0:T(8,128)S(1)}, u32[]{:S(2)}, u32[]{:S(2)}) async-start(f32[8,1216,56]{1,2,0:T(8,128)} %bitcast.31), calls=%async_computation.6 | async-start | bytes 4587520 | tf_op jit(solution)/shard_map/all_to_all | solution.py:34
  187.7 30.3 %copy-start.2 = (bf16[1024,448]{0,1:T(8,128)(2,1)S(1)}, bf16[1024,448]{0,1:T(8,128)(2,1)}, u32[]{:S(2)}) copy-start(bf16[1024,448]{0,1:T(8,128)(2,1)} %param.13) | copy-start | bytes 2752516
where the time goes:
time: 297 us; the launch traced here: 292 us
  blocking collectives  171 us (58%)
  waiting for transfers between devices  59.3 us (20%)
  local copies, waits for them, and re-layouts  23.4 us (8%)
  starting transfers between devices  15.8 us (5%)
  other arithmetic  13.2 us (4%)
  matrix products  8.71 us (3%)
    all_to_all x4, blocking collectives, copy_for_each(): lax.all_to_all(jnp.broadcast_to(x[None], (size, *x.shape)), axis, 0, 0, t...  79.1 us
    all_to_all x1, blocking collectives, sum_in_two_steps(): return jnp.sum(lax.all_to_all(own, far, 0, 0, tiled=True), axis=0)  56.8 us
    all_to_all x1, waiting for transfers between devices, summed_on_arrival(): lax.all_to_all(blocks, axis, split_axis=0, concat_axis=0, tiled=True)  32.7 us
    all_to_all x2, waiting for transfers between devices, copy_for_each(): lax.all_to_all(jnp.broadcast_to(x[None], (size, *x.shape)), axis, 0, 0, t...  26.6 us
    all_gather x1, blocking collectives, turned_gather(): out = lax.all_gather(both, axis, axis=0, tiled=True)  23.3 us
    transpose x2, other arithmetic, turned_gather(): turned = [jnp.moveaxis(a, dim, 0) for a, dim in zip(arrays, dims)]  12.1 us
    all_to_all x1, blocking collectives, summed_on_arrival(): lax.all_to_all(blocks, axis, split_axis=0, concat_axis=0, tiled=True)  11.9 us
    all_to_all x2, starting transfers between devices, copy_for_each(): lax.all_to_all(jnp.broadcast_to(x[None], (size, *x.shape)), axis, 0, 0, t...  11.5 us
  transfers between devices with their start and end apart: 3, of which 3 were waited for; matrix products, arithmetic and copies ran while one was open for 3% of the time, Pallas kernels for 0%

commit v1 on v0

v1 whole, which is shorter than its diff:
```python
import functools

import jax
import jax.numpy as jnp
import numpy as np
from jax import lax
from jax.experimental import pallas as pl
from jax.experimental.pallas import tpu as pltpu
from jax.sharding import Mesh
from jax.sharding import PartitionSpec as P

MESH = pl.DeviceIdType.MESH
BF = jnp.bfloat16
F32 = jnp.float32
Z = 16
NT = (((1,), (1,)), ((), ()))


def dot(a, b):
    return jnp.dot(a, b, preferred_element_type=F32)


def dot_nt(a, b):
    return lax.dot_general(a, b, NT, preferred_element_type=F32)


def slot_offset(p):
    return -((p + 1) // 2) if p % 2 else p // 2


def compact_rows():
    s = np.zeros((48, 64), np.float32)
    for m in range(4):
        for r in range(12):
            s[m * 12 + r, m * 16 + r] = 1
    return s


def chunk_rows():
    s = np.zeros((208, 192), np.float32)
    for q in range(4):
        for h in range(2):
            for c in range(2):
                base = 48 * q + (2 * h + c) * 12
                for i in range(2):
                    s[q * 8 + h * 4 + c * 2 + i, base + 10 + i] = 1
                for i in range(5):
                    s[32 + h * 40 + q * 10 + c * 5 + i, base + i] = 1
                    s[112 + h * 48 + q * 10 + c * 5 + i, base + 5 + i] = 1
    return s


def pack_rows():
    s = np.zeros((384, 320), np.float32)
    for p in range(8):
        for t in range(4):
            for i in range(10):
                s[p * 48 + 10 * t + i, 80 * t + 10 * p + i] = 1
    return s


def row_table():
    t = np.zeros((160, 128), np.int32)
    for r in range(160):
        t[r, 0] = slot_offset(r // 10)
        t[r, 1] = r % 10
    return t


def kernel(
    ex_ref, rf_ref, ct_ref, wg_hbm, wu_hbm, wd_hbm, pair_ref, points_ref,
    sel0_ref, sel_ref, pack_ref, table_ref,
    out_ref,
    wg, wu, wd, wcat, wd2, tile, quad, xbuf, xs, sendb, recvb, onehot, base, accr, acce, accu,
    bdiag, sendc, full, d1send, d1recv, keep, d2send, d2recv, d3send, d3recv, fin, finr,
    wsem, qs, qr, zs, zr, ms, mr, bs, br, cs, cr, d1s, d1r, d2s, d2r, d3s, d3r, fs, fr,
):
    h, z, c = lax.axis_index("h"), lax.axis_index("z"), lax.axis_index("c")
    x, l = lax.axis_index("x"), lax.axis_index("l")
    mine = 2 * x + l
    pending = []

    def send(src, dst, ssem, rsem, dev):
        cp = pltpu.make_async_remote_copy(
            src_ref=src, dst_ref=dst, send_sem=ssem, recv_sem=rsem, device_id=dev, device_id_type=MESH
        )
        cp.start()
        pending.append(cp)
        return cp

    loads = [
        pltpu.make_async_copy(a, b, wsem.at[i])
        for i, (a, b) in enumerate(((wg_hbm, wg), (wu_hbm, wu), (wd_hbm, wd)))
    ]
    for cp in loads:
        cp.start()

    quads = [{"h": lax.rem(h + i // 2, 2), "c": lax.rem(c + i % 2, 2)} for i in range(4)]
    peers = [{"x": lax.rem(x + i // 2, 4), "l": lax.rem(l + i % 2, 2)} for i in range(8)]
    alongz = [{"z": lax.rem(z + slot_offset(p) + Z, Z)} for p in range(Z)]
    barrier = pltpu.get_barrier_semaphore()
    for dev in quads[1:] + peers[1:] + alongz[1:]:
        pl.semaphore_signal(barrier, inc=1, device_id=dev, device_id_type=MESH)

    t = jnp.concatenate(
        [ex_ref[...].astype(F32), ct_ref[...].astype(F32), rf_ref[...].astype(F32), jnp.zeros((4, 1024), F32)], axis=0
    ).astype(BF)
    tile[...] = t
    m = 2 * h + c
    quad[m] = t
    pl.semaphore_wait(barrier, 25)
    qcopies = [send(tile, quad.at[m], qs.at[i], qr.at[i], quads[i]) for i in range(1, 4)]

    for cp in loads:
        cp.wait()

    def prep(a):
        w0 = (0, 0, 128, 256)[a]
        kk = min(256, 448 - w0)
        k = lax.broadcasted_iota(jnp.int32, (kk, 256), 0) + w0
        n = lax.broadcasted_iota(jnp.int32, (kk, 256), 1)
        r = n & 127
        first = 56 * (2 * a + (n >> 7))
        sg = jnp.where((r < 56) & (k == first + r), 1.0, 0.0).astype(BF)
        su = jnp.where((r >= 64) & (r < 120) & (k == first + r - 64), 1.0, 0.0).astype(BF)
        for b in range(4):
            rows = pl.ds(256 * b, 256)
            wcat[rows, pl.ds(256 * a, 256)] = (
                dot(wg[rows, pl.ds(w0, kk)], sg) + dot(wu[rows, pl.ds(w0, kk)], su)
            ).astype(BF)
        k = lax.broadcasted_iota(jnp.int32, (256, kk), 1) + w0
        n = lax.broadcasted_iota(jnp.int32, (256, kk), 0)
        r = n & 63
        sd = jnp.where((r < 56) & (k == 56 * (2 * a + (n >> 7)) + r), 1.0, 0.0).astype(BF)
        for b in range(4):
            cols = pl.ds(256 * b, 256)
            wd2[pl.ds(256 * a, 256), cols] = dot(sd, wd[pl.ds(w0, kk), cols]).astype(BF)

    prep(0)

    for cp in qcopies:
        cp.wait_recv()
    xbuf[0] = dot(sel0_ref[...], quad[...].reshape(64, 1024)).astype(BF)

    onward = {"z": lax.rem(z + 1 - 2 * c + Z, Z)}
    mate = {"c": 1 - c}

    def own_slot(s):
        return 2 * s - 1 + (c if s < 8 else 0)

    def columns(s, u):
        return pl.ds(pl.multiple_of((512 * c) if s == 8 else 512 * u, 512), 512)

    def zcopy(s, u):
        src = xbuf.at[0 if s == 1 else own_slot(s - 1), :, columns(s, u)]
        return send(src, xbuf.at[own_slot(s), :, columns(s, u)], zs.at[2 * s + u], zr.at[2 * s + u], onward)

    def mcopy(s, u):
        at = xbuf.at[own_slot(s), :, columns(s, u)]
        return send(at, at, ms.at[2 * s + u], mr.at[2 * s + u], mate)

    def work(k):
        xs[...] = dot(sel_ref[...], xbuf[4 * k : 4 * k + 4].reshape(192, 1024)).astype(BF)
        left = lax.broadcasted_iota(jnp.int32, (48, 256), 1) & 127

        @pl.loop(0, 4)
        def _(n):
            cols = pl.ds(pl.multiple_of(256 * n, 256), 256)
            p = dot(xs[0:112], wcat[:, cols]).astype(BF)
            d = dot_nt(xs[112:208], wd2[cols, :])
            d = jnp.where(left < 64, d[:48], d[48:]).astype(BF)
            for e in range(2):
                sendb[k, 2 * n + e, 0:112] = p[:, 128 * e : 128 * e + 128]
                sendb[k, 2 * n + e, 112:160] = d[:, 128 * e : 128 * e + 128]

        for i in range(1, 8):
            j = 2 * lax.rem(x + i // 2, 4) + lax.rem(l + i % 2, 2)
            bcopies[k, i] = send(sendb.at[k, j], recvb.at[k, i], bs.at[8 * k + i], br.at[8 * k + i], peers[i])

    bcopies, done = {}, {}
    zc = {(1, u): zcopy(1, u) for u in range(2)}
    mc = {}

    def choose():
        off, place = table_ref[:, 0:1], table_ref[:, 1:2]
        want = ((z + off + Z) & (Z - 1)) * 10 + place
        perm = jnp.where(lax.broadcasted_iota(jnp.int32, (160, 160), 1) == want, 1.0, 0.0).astype(BF)
        for hh in range(2):
            rows = pair_ref[160 * hh : 160 * hh + 160, :].astype(F32).astype(BF)
            r = dot(perm, rows).astype(jnp.int32)
            delta = (((r >> 2) & 15) - z + Z) & (Z - 1)
            slot = jnp.where(delta < 8, 2 * delta, 2 * (Z - delta) - 1)
            pos = slot * 8 + (r >> 6) * 4 + (r & 3)
            lane = lax.broadcasted_iota(jnp.int32, (160, 128), 1)
            for p in range(4):
                onehot[p, :, 128 * hh : 128 * hh + 128] = jnp.where(lane == pos[:, p : p + 1], 1.0, 0.0).astype(BF)

    for s in range(1, 9):
        for u in range(2 if s < 8 else 1):
            zc[s, u].wait_recv()
            if s < 7 or (s == 7 and u == 1):
                for v in ([u] if s < 7 else [0]):
                    zc[s + 1, v] = zcopy(s + 1, v)
            mc[s, u] = mcopy(s, u)
        if s < 4:
            prep(s)
        if s == 4:
            choose()
        if s >= 4:
            k = s - 4
            if k < 3:
                pass
        if s in (4, 6, 7):
            k = {4: 0, 6: 1, 7: 2}[s]
            for q in range(1, 2 * k + 3):
                for u in range(2):
                    if not done.get((q, u)):
                        done[q, u] = True
                        mc[q, u].wait_recv()
            work(k)
    for q in range(1, 9):
        for u in range(2 if q < 8 else 1):
            if not done.get((q, u)):
                done[q, u] = True
                mc[q, u].wait_recv()
    work(3)

    lane = lax.broadcasted_iota(jnp.int32, (160, 128), 1)
    for k in range(4):
        total = sendb[k, mine].astype(F32)
        for i in range(1, 8):
            bcopies[k, i].wait_recv()
            total = total + recvb[k, i].astype(F32)
        accr[32 * k : 32 * k + 32] = total[0:32]
        e0, e1 = total[32:72], total[72:112]
        half = lane[:40] < 64
        acce[0, 40 * k : 40 * k + 40] = jnp.where(half, e0, pltpu.roll(e1, 64, 1))
        acce[1, 40 * k : 40 * k + 40] = jnp.where(half, pltpu.roll(e0, 64, 1), e1)
        accu[40 * k : 40 * k + 40] = total[112:152]

    refs = accr[...]
    turned = pltpu.roll(refs, 64, 1)
    left = lane[:128] < 64
    diag = (
        jnp.where(left, refs, 0.0), jnp.where(left, 0.0, turned),
        jnp.where(left, turned, 0.0), jnp.where(left, 0.0, refs),
    )
    for n, block in enumerate(diag):
        high = block.astype(BF)
        low = (block - high.astype(F32)).astype(BF)
        at = (slice(128 * (n % 2), 128 * (n % 2) + 128), slice(128 * (n // 2), 128 * (n // 2) + 128))
        bdiag[(0, *at)] = high
        bdiag[(1, *at)] = low
    for p in range(4):
        base[p] = dot(onehot[p], bdiag[0]) + dot(onehot[p], bdiag[1])

    alphas = [points_ref[i].astype(F32) * 0.125 for i in range(8)]

    @pl.loop(0, 5)
    def _(n):
        rows = pl.ds(pl.multiple_of(32 * n, 32), 32)
        eg, eu, up = acce[0, rows], acce[1, rows], accu[rows]
        cg = jnp.zeros((32, 128), F32)
        cu = jnp.zeros((32, 128), F32)
        for p in range(4):
            bg, bu = base[p, rows, 0:128], base[p, rows, 128:256]
            dg, du = eg - bg, eu - bu
            for a in alphas:
                g = bg + a * dg
                u = bu + a * du
                s = 0.5 * jnp.tanh(0.5 * g) + 0.5
                gs = g * s
                cu = cu + gs
                cg = cg + u * (s + gs * (1.0 - s))
        cg = up * (cg * (1.0 / 32.0))
        cu = up * (cu * (1.0 / 32.0))
        half = lax.broadcasted_iota(jnp.int32, (32, 128), 1) < 64
        sendc[rows, :] = jnp.where(half, cg, pltpu.roll(cu, 64, 1)).astype(BF)
        sendc[pl.ds(pl.multiple_of(160 + 32 * n, 32), 32), :] = jnp.where(half, pltpu.roll(cg, 64, 1), cu).astype(BF)

    lanes = pl.ds(pl.multiple_of(128 * mine, 128), 128)
    ccopies = [send(sendc, full.at[:, lanes], cs.at[i], cr.at[i], peers[i]) for i in range(1, 8)]
    full[:, lanes] = sendc[...]
    for cp in ccopies:
        cp.wait_recv()

    def product(hh, cc, into, at):
        rows = pl.ds(pl.multiple_of(160 * hh, 160), 160)

        @pl.loop(0, 2)
        def _(n):
            w = pl.ds(pl.multiple_of(512 * cc + 256 * n, 256), 256)
            into[at, :, pl.ds(pl.multiple_of(256 * n, 256), 256)] = dot_nt(full[rows, :], wcat[w, :])

    d1 = []
    product(1 - h, 1 - c, d1send, 0)
    d1.append(send(d1send.at[0], d1recv.at[0], d1s.at[0], d1r.at[0], mate))
    product(1 - h, c, keep, 0)
    d1[0].wait_recv()
    d2send[...] = (keep[0] + d1recv[0]).astype(BF)
    d2 = send(d2send, d2recv, d2s, d2r, {"h": 1 - h})
    product(h, 1 - c, d1send, 1)
    d1.append(send(d1send.at[1], d1recv.at[1], d1s.at[1], d1r.at[1], mate))
    product(h, c, keep, 1)
    d1[1].wait_recv()
    keep[1] = keep[1] + d1recv[1]
    d2.wait_recv()
    d3 = []
    for g in range(2):
        rows = slice(80 * g, 80 * g + 80)
        v = (keep[1, rows] + d2recv[rows].astype(F32)).astype(BF)
        v = jnp.concatenate([v[:, 128 * t : 128 * t + 128] for t in range(4)], axis=0)
        d3send[8 * g : 8 * g + 8] = dot(pack_ref[...], v).astype(BF).reshape(8, 48, 128)
        for p in range(8 * g, 8 * g + 8):
            if p:
                d3.append(send(d3send.at[p], d3recv.at[p], d3s.at[p], d3r.at[p], alongz[p]))
    total = d3send[0].astype(F32)
    for p in range(1, Z):
        d3[p - 1].wait_recv()
        total = total + d3recv[p].astype(F32)
    fin[...] = total
    last = send(fin, finr, fs, fr, mate)
    last.wait_recv()
    other = finr[...]
    first = c == 0
    parts = []
    for block in (jnp.where(first, total, other), jnp.where(first, other, total)):
        for t in range(4):
            parts.append(jnp.where(first, block[10 * t : 10 * t + 5], block[10 * t + 5 : 10 * t + 10]))
    out_ref[...] = jnp.concatenate(parts, axis=1).astype(BF)
    for cp in pending:
        cp.wait_send()


def on_device(examples, references, gate_weight, up_weight, down_weight, cotangent, pair_ref, points):
    vm = pl.BlockSpec(memory_space=pltpu.VMEM)
    hbm = pl.BlockSpec(memory_space=pl.ANY)
    sm = pl.BlockSpec(memory_space=pltpu.SMEM)
    dma = pltpu.SemaphoreType.DMA
    V = pltpu.VMEM
    return pl.pallas_call(
        kernel,
        out_shape=jax.ShapeDtypeStruct((5, 1024), BF),
        in_specs=[vm, vm, vm, hbm, hbm, hbm, vm, sm, vm, vm, vm, vm],
        out_specs=vm,
        scratch_shapes=[
            V((1024, 448), BF), V((1024, 448), BF), V((448, 1024), BF),
            V((1024, 1024), BF), V((1024, 1024), BF),
            V((16, 1024), BF), V((4, 16, 1024), BF), V((Z, 48, 1024), BF), V((208, 1024), BF),
            V((4, 8, 160, 128), BF), V((4, 8, 160, 128), BF),
            V((4, 160, 256), BF), V((4, 160, 256), F32),
            V((128, 128), F32), V((2, 160, 128), F32), V((160, 128), F32),
            V((2, 256, 256), BF), V((320, 128), BF), V((320, 1024), BF),
            V((2, 160, 512), F32), V((2, 160, 512), F32), V((2, 160, 512), F32),
            V((160, 512), BF), V((160, 512), BF),
            V((Z, 48, 128), BF), V((Z, 48, 128), BF), V((48, 128), F32), V((48, 128), F32),
            dma((3,)), dma((4,)), dma((4,)), dma((18,)), dma((18,)), dma((18,)), dma((18,)),
            dma((32,)), dma((32,)), dma((8,)), dma((8,)), dma((2,)), dma((2,)), dma, dma,
            dma((Z,)), dma((Z,)), dma, dma,
        ],
        compiler_params=pltpu.CompilerParams(
            collective_id=0, has_side_effects=True, vmem_limit_bytes=48 * 1024 * 1024
        ),
        cost_estimate=pl.CostEstimate(flops=2 * 10**9, bytes_accessed=4 * 10**6, transcendentals=10**6),
    )(
        examples, references, cotangent, gate_weight, up_weight, down_weight, pair_ref, points,
        jnp.asarray(compact_rows(), BF), jnp.asarray(chunk_rows(), BF),
        jnp.asarray(pack_rows(), BF), jnp.asarray(row_table()),
    )


def solution(mesh):
    split = Mesh(mesh.devices.reshape(2, Z, 2, 4, 2), ("h", "z", "c", "x", "l"))
    wide, narrow = ("h", "z", "c"), ("x", "l")
    return jax.shard_map(
        on_device,
        mesh=split,
        in_specs=(
            P(wide, narrow), P(wide, narrow), P(narrow, wide), P(narrow, wide),
            P(wide, narrow), P(wide, narrow), P(), P(),
        ),
        out_specs=P(wide, narrow),
        check_vma=False,
    )
```

time: 297 us -> 101 us (0.34); the launches traced: 292 us -> 100 us
  blocking collectives: 171 us -> 0 us
  Pallas kernels: 0 us -> 93.9 us
  waiting for transfers between devices: 59.3 us -> 0 us
  local copies, waits for them, and re-layouts: 23.4 us -> 6.26 us
  starting transfers between devices: 15.8 us -> 0 us
  other arithmetic: 13.2 us -> 0 us
  matrix products: 8.71 us -> 0 us
    all_to_all x6 -> x0, blocking collectives: 148 us -> none  [the longest x4 79.1 us: copy_for_each(): lax.all_to_all(jnp.broadcast_to(x[None], (size, *x.shape)), axis, 0, 0, t...]
    pallas_call x0 -> x1, Pallas kernels: none -> 93.9 us  [on_device(): pl.pallas_call(kernel, out_shape=jax.ShapeDtypeStruct((5, 1024), BF), in_...]
    all_to_all x3 -> x0, waiting for transfers between devices: 59.3 us -> none  [the longest x1 32.7 us: summed_on_arrival(): lax.all_to_all(blocks, axis, split_axis=0, concat_axis=0, tiled=True)]
    all_gather x1 -> x0, blocking collectives: 23.3 us -> none  [turned_gather(): out = lax.all_gather(both, axis, axis=0, tiled=True)]
    all_to_all x3 -> x0, starting transfers between devices: 15.8 us -> none  [the longest x2 11.5 us: copy_for_each(): lax.all_to_all(jnp.broadcast_to(x[None], (size, *x.shape)), axis, 0, 0, t...]
    transpose x2 -> x0, other arithmetic: 12.1 us -> none  [turned_gather(): turned = [jnp.moveaxis(a, dim, 0) for a, dim in zip(arrays, dims)]]
    gather x16 -> x0, local copies, waits for them, and re-layouts: 9.57 us -> none  [the longest x8 4.79 us: path_coefficients(): base_up = jnp.take(reference_up, chosen, axis=0)]
    dot_general x7 -> x0, matrix products: 8.71 us -> none  [the longest x3 3.65 us: transposed_product(): lax.dot_general(left, right, (((1,), (1,)), ((), ())), preferred_element_...]
  transfers between devices with their start and end apart: 3 -> 0, of which waited for: 3 -> 0; matrix products, arithmetic and copies ran while one was open for 3% -> 0% of each run, Pallas kernels for 0% -> 0%
where the time goes in v1:
time: 101 us; the launch traced here: 100 us
  Pallas kernels  93.9 us (93%)
  local copies, waits for them, and re-layouts  6.26 us (6%)
    pallas_call x1, Pallas kernels, on_device(): pl.pallas_call(kernel, out_shape=jax.ShapeDtypeStruct((5, 1024), BF), in_...  93.9 us
    unnamed x22, local copies, waits for them, and re-layouts  6.26 us

profile of v1, /device:TPU:1, one launch (start us, length us, event | category | flops | bytes accessed | tf_op | source)
XLA Modules:
  0.0 100.3 jit_solution(10605142739991421571)
XLA Ops:
  0.0 0.8 copy.15.pair_ref
  0.8 1.5 %copy.13.wg_hbm = bf16[1024,448]{1,0:T(8,128)(2,1)S(1)} copy(bf16[1024,448]{0,1:T(8,128)(2,1)} %param.14) | data formatting | bytes 1835008 | tf_op args[2]
  2.3 0.0 copy-start
  2.3 0.0 copy-start.1
  2.3 0.0 copy-start.2
  2.3 0.0 copy-start.3
  2.4 0.0 copy-start.4
  2.4 0.0 copy-start.5
  2.4 0.0 copy-start.8
  2.4 1.5 %copy.14.wu_hbm = bf16[1024,448]{1,0:T(8,128)(2,1)S(1)} copy(bf16[1024,448]{0,1:T(8,128)(2,1)} %param.15) | data formatting | bytes 1835008 | tf_op args[3]
  3.9 0.0 copy-done
  4.0 0.0 copy-done.1
  4.0 0.0 copy-done.2
  4.0 0.0 copy-done.3
  4.0 0.0 copy-done.4
  4.0 0.0 copy-done.5
  4.0 0.0 copy-done.8
  4.0 0.0 copy-start.6
  4.0 0.9 copy-done.6
  4.9 0.0 copy-start.7
  4.9 0.9 copy-done.7
  5.8 93.9 %shard_map.118 = bf16[5,1024]{1,0:T(8,128)(2,1)S(1)} custom-call(bf16[5,1024]{1,0:T(8,128)(2,1)S(1)} %copy-done.1, bf16[2,1024]{1,0:T(2,128)(2,1)S(1)} %copy-done.3, bf16[5,1024]{1,0:T(8,128)(2,1)S(1)} %copy-done.2, bf16[1024,448]{1,0:T(8,128)(2,1)S(1)} %copy.13.wg_hbm, bf16[1024,448]{1,0:T(8,128)(2,1)S(1)} %copy.14.wu_hbm, bf16[448,1024]{1,0:T(8,128)(2,1)S(1)} %copy-done, ...), custom_call_target="tpu_custom_call" | custom-call | flops 2000000000 | bytes 4000000 | tf_op jit(solution)/shard_map/pallas_call | solution.py:341
  99.7 0.6 copy.17
Async XLA Ops:
  2.3 1.6 %copy-start = (bf16[448,1024]{1,0:T(8,128)(2,1)S(1)}, bf16[448,1024]{1,0:T(8,128)(2,1)}, u32[]{:S(2)}) copy-start(bf16[448,1024]{1,0:T(8,128)(2,1)} %wd_hbm.1) | copy-start | bytes 2752516
  2.3 1.6 %copy-start.1 = (bf16[5,1024]{1,0:T(8,128)(2,1)S(1)}, bf16[5,1024]{1,0:T(8,128)(2,1)}, u32[]{:S(2)}) copy-start(bf16[5,1024]{1,0:T(8,128)(2,1)} %ex_ref.1) | copy-start | bytes 30724
  2.3 1.6 %copy-start.2 = (bf16[5,1024]{1,0:T(8,128)(2,1)S(1)}, bf16[5,1024]{1,0:T(8,128)(2,1)}, u32[]{:S(2)}) copy-start(bf16[5,1024]{1,0:T(8,128)(2,1)} %ct_ref.1) | copy-start | bytes 30724
  2.3 1.6 %copy-start.3 = (bf16[2,1024]{1,0:T(2,128)(2,1)S(1)}, bf16[2,1024]{1,0:T(2,128)(2,1)}, u32[]{:S(2)}) copy-start(bf16[2,1024]{1,0:T(2,128)(2,1)} %rf_ref.1) | copy-start | bytes 12292
  2.4 1.6 %copy-start.4 = (s32[8]{0:T(128)S(1)}, s32[8]{0:T(128)}, u32[]{:S(2)}) copy-start(s32[8]{0:T(128)} %points_ref.1) | copy-start | bytes 100
  2.4 1.6 %copy-start.5 = (bf16[384,320]{1,0:T(8,128)(2,1)S(1)}, bf16[384,320]{1,0:T(8,128)(2,1)}, u32[]{:S(2)}) copy-start(bf16[384,320]{1,0:T(8,128)(2,1)} %constant.10.clone.pack_ref) | copy-start | bytes 737284
  2.4 1.6 %copy-start.8 = (bf16[48,64]{1,0:T(8,128)(2,1)S(1)}, bf16[48,64]{1,0:T(8,128)(2,1)}, u32[]{:S(2)}) copy-start(bf16[48,64]{1,0:T(8,128)(2,1)} %constant.8.clone.sel0_ref) | copy-start | bytes 18436
  4.0 0.9 copy-start.6
  4.9 0.9 copy-start.7

commit v2 on v1

v2 whole, which is shorter than its diff:
```python
import functools

import jax
import jax.numpy as jnp
import numpy as np
from jax import lax
from jax.experimental import pallas as pl
from jax.experimental.pallas import tpu as pltpu
from jax.sharding import Mesh
from jax.sharding import PartitionSpec as P

MESH = pl.DeviceIdType.MESH
BF = jnp.bfloat16
F32 = jnp.float32
Z = 16
NT = (((1,), (1,)), ((), ()))


def dot(a, b):
    return jnp.dot(a, b, preferred_element_type=F32)


def dot_nt(a, b):
    return lax.dot_general(a, b, NT, preferred_element_type=F32)


OFFSETS = (0, 1, -1, 2, -2, 4, -4, 8, 3, -3, 5, -5, 6, -6, 7, -7)


def slot_of(offset):
    return next(p for p in range(Z) if (OFFSETS[p] - offset) % Z == 0)


def compact_rows():
    s = np.zeros((48, 64), np.float32)
    for m in range(4):
        for r in range(12):
            s[m * 12 + r, m * 16 + r] = 1
    return s


def chunk_rows():
    s = np.zeros((4, 208, 768), np.float32)
    for t in range(4):
        for q in range(4):
            for h in range(2):
                for c in range(2):
                    base = 48 * (4 * (2 * h + c) + q) + 12 * t
                    for i in range(2):
                        s[t, q * 8 + h * 4 + c * 2 + i, base + 10 + i] = 1
                    for i in range(5):
                        s[t, 32 + h * 40 + q * 10 + c * 5 + i, base + i] = 1
                        s[t, 112 + h * 48 + q * 10 + c * 5 + i, base + 5 + i] = 1
    return s


def pack_rows():
    s = np.zeros((384, 320), np.float32)
    for p in range(8):
        for t in range(4):
            for i in range(10):
                s[p * 48 + 10 * t + i, 80 * t + 10 * p + i] = 1
    return s


def row_table():
    t = np.zeros((160, 128), np.int32)
    for r in range(160):
        t[r, 0] = OFFSETS[r // 10]
        t[r, 1] = r % 10
    return t


def kernel(
    ex_ref, rf_ref, ct_ref, wg_hbm, wu_hbm, wd_hbm, pair_ref, points_ref,
    sel0_ref, sel_hbm, pack_hbm, table_ref,
    out_ref,
    wg, wu, wd, sel, pack, wcat, wd2, xbuf, xs, sendb, recvb, keepb, lsend, lrecv, onehot, base, accr, acce, accu,
    bdiag, sendc, full, d1send, d1recv, keep, d2send, d2recv, d3send, d3recv, fin, finr,
    wsem, zs, zr, hs, hr, ms, mr, gs, gr, bs, br, ls, lr, cs, cr, d1s, d1r, d2s, d2r, d3s, d3r, fs, fr,
):
    h, z, c = lax.axis_index("h"), lax.axis_index("z"), lax.axis_index("c")
    x, l = lax.axis_index("x"), lax.axis_index("l")
    mine = 2 * x + l
    m, mh = 2 * h + c, 2 * (1 - h) + c
    pending = []

    def send(src, dst, ssem, rsem, dev):
        cp = pltpu.make_async_remote_copy(
            src_ref=src, dst_ref=dst, send_sem=ssem, recv_sem=rsem, device_id=dev, device_id_type=MESH
        )
        cp.start()
        pending.append(cp)
        return cp

    def along(offset):
        return {"z": lax.rem(z + offset + Z, Z)}

    facing, mate, beside = {"h": 1 - h}, {"c": 1 - c}, {"l": 1 - l}
    row = [{"x": lax.rem(x + i, 4)} for i in range(4)]
    peers = [{"x": lax.rem(x + i // 2, 4), "l": lax.rem(l + i % 2, 2)} for i in range(8)]
    barrier = pltpu.get_barrier_semaphore()
    for dev in [along(e) for e in (8, 4, -4, 2, -2, 1, -1)] + [facing] + row[1:] + [beside, mate]:
        pl.semaphore_signal(barrier, inc=1, device_id=dev, device_id_type=MESH)

    loads = [
        pltpu.make_async_copy(a, b, wsem.at[i])
        for i, (a, b) in enumerate(((wg_hbm, wg), (wu_hbm, wu), (wd_hbm, wd), (sel_hbm, sel), (pack_hbm, pack)))
    ]
    for cp in loads:
        cp.start()

    t = jnp.concatenate(
        [ex_ref[...].astype(F32), ct_ref[...].astype(F32), rf_ref[...].astype(F32), jnp.zeros((4, 1024), F32)], axis=0
    ).astype(BF)
    t = jnp.concatenate([t[:, 256 * i : 256 * i + 256] for i in range(4)], axis=0)
    xbuf[0, m, 0] = dot(sel0_ref[...], t).astype(BF)
    pl.semaphore_wait(barrier, 13)

    def block(p):
        return xbuf.at[p // 4, m, p % 4]

    zc = {}

    def zsend(offset, e):
        p = slot_of(offset - e)
        zc[p] = send(block(slot_of(offset)), block(p), zs.at[p], zr.at[p], along(e))

    for e in (8, 4, -4, 2, -2, 1, -1):
        zsend(0, e)

    for cp in loads:
        cp.wait()

    def prep(a):
        w0 = (0, 0, 128, 256)[a]
        kk = min(256, 448 - w0)
        k = lax.broadcasted_iota(jnp.int32, (256, kk), 1) + w0
        n = lax.broadcasted_iota(jnp.int32, (256, kk), 0)
        r = n & 127
        first = 56 * (2 * a + (n >> 7))
        gate = (r < 56) & (k == first + r)
        up = (r >= 64) & (r < 120) & (k == first + r - 64)
        sg = jnp.where(gate, 1.0, 0.0).astype(BF)
        su = jnp.where(up, 1.0, 0.0).astype(BF)
        sd = jnp.where(gate | up, 1.0, 0.0).astype(BF)
        for b in range(4):
            cols = pl.ds(256 * b, 256)
            rows = pl.ds(w0, kk)
            wcat[pl.ds(256 * a, 256), cols] = (dot(sg, wg[rows, cols]) + dot(su, wu[rows, cols])).astype(BF)
            wd2[pl.ds(256 * a, 256), cols] = dot(sd, wd[rows, cols]).astype(BF)

    hc, mc, gc = {}, {}, {}

    def spread(k):
        for q in range(4):
            if 4 * k + q and 4 * k + q not in (5, 6, 7):
                zc[4 * k + q].wait_recv()
        at = xbuf.at[k, m]
        hc[k] = send(at, at, hs.at[k], hr.at[k], facing)
        mc[k] = send(at, at, ms.at[k], mr.at[k], mate)

    def onward(k):
        hc[k].wait_recv()
        at = xbuf.at[k, mh]
        gc[k] = send(at, at, gs.at[k], gr.at[k], mate)

    def work(k):
        mc[k].wait_recv()
        gc[k].wait_recv()
        blocks = xbuf[k].reshape(768, 256)
        for i in range(4):
            xs[:, 256 * i : 256 * i + 256] = dot(sel[i], blocks).astype(BF)
        left = lax.broadcasted_iota(jnp.int32, (48, 256), 1) & 127

        @pl.loop(0, 4)
        def _(n):
            cols = pl.ds(pl.multiple_of(256 * n, 256), 256)
            p = dot_nt(xs[0:112], wcat[cols, :]).astype(BF)
            d = dot_nt(xs[112:208], wd2[cols, :])
            d = jnp.where(left < 64, d[:48], d[48:]).astype(BF)
            for e in range(2):
                sendb[k, n, e, 0:112] = p[:, 128 * e : 128 * e + 128]
                sendb[k, n, e, 112:160] = d[:, 128 * e : 128 * e + 128]

        for i in range(1, 4):
            bc[k, i] = send(
                sendb.at[k, lax.rem(x + i, 4)], recvb.at[k, i], bs.at[4 * k + i], br.at[4 * k + i], row[i]
            )

    bc, lc = {}, {}

    def owner_sum(k):
        for i in range(1, 4):
            bc[k, i].wait_recv()
        theirs = sendb[k, x, 1 - l].astype(F32)
        for i in range(1, 4):
            theirs = theirs + recvb[k, i, 1 - l].astype(F32)
        lsend[k] = theirs
        lc[k] = send(lsend.at[k], lrecv.at[k], ls.at[k], lr.at[k], beside)
        ours = sendb[k, x, l].astype(F32)
        for i in range(1, 4):
            ours = ours + recvb[k, i, l].astype(F32)
        keepb[k] = ours

    def owner_end(k):
        lc[k].wait_recv()
        total = keepb[k] + lrecv[k]
        accr[32 * k : 32 * k + 32] = total[0:32]
        e0, e1 = total[32:72], total[72:112]
        half = lax.broadcasted_iota(jnp.int32, (40, 128), 1) < 64
        acce[0, 40 * k : 40 * k + 40] = jnp.where(half, e0, pltpu.roll(e1, 64, 1))
        acce[1, 40 * k : 40 * k + 40] = jnp.where(half, pltpu.roll(e0, 64, 1), e1)
        accu[40 * k : 40 * k + 40] = total[112:152]

    def choose():
        off, place = table_ref[:, 0:1], table_ref[:, 1:2]
        want = ((z + off + Z) & (Z - 1)) * 10 + place
        perm = jnp.where(lax.broadcasted_iota(jnp.int32, (160, 160), 1) == want, 1.0, 0.0).astype(BF)
        for hh in range(2):
            picks = pair_ref[...].astype(F32)[:, 160 * hh : 160 * hh + 160].astype(BF)
            r = dot_nt(perm, picks).astype(jnp.int32)
            delta = (((r >> 2) & 15) - z + Z) & (Z - 1)
            slot = jnp.zeros_like(delta)
            for p in range(1, Z):
                slot = jnp.where(delta == OFFSETS[p] % Z, p, slot)
            pos = slot * 8 + (r >> 6) * 4 + (r & 3)
            lane = lax.broadcasted_iota(jnp.int32, (160, 128), 1)
            for p in range(4):
                onehot[p, :, 128 * hh : 128 * hh + 128] = jnp.where(lane == pos[:, p : p + 1], 1.0, 0.0).astype(BF)

    prep(0)
    prep(1)
    for p in (7, 5, 6):
        zc[p].wait_recv()
        for offset, e in {7: ((8, 1), (8, -1)), 5: ((4, -2), (4, 1), (4, -1)), 6: ((-4, 2), (-4, 1), (-4, -1))}[p]:
            zsend(offset, e)
    spread(0)
    spread(1)
    prep(2)
    prep(3)
    onward(0)
    onward(1)
    work(0)
    spread(2)
    work(1)
    spread(3)
    choose()
    onward(2)
    owner_sum(0)
    work(2)
    onward(3)
    owner_sum(1)
    work(3)
    owner_end(0)
    owner_sum(2)
    owner_end(1)
    owner_sum(3)
    owner_end(2)
    owner_end(3)

    lane = lax.broadcasted_iota(jnp.int32, (160, 128), 1)
    refs = accr[...]
    turned = pltpu.roll(refs, 64, 1)
    left = lane[:128] < 64
    diag = (
        jnp.where(left, refs, 0.0), jnp.where(left, 0.0, turned),
        jnp.where(left, turned, 0.0), jnp.where(left, 0.0, refs),
    )
    for n, block in enumerate(diag):
        high = block.astype(BF)
        low = (block - high.astype(F32)).astype(BF)
        at = (slice(128 * (n % 2), 128 * (n % 2) + 128), slice(128 * (n // 2), 128 * (n // 2) + 128))
        bdiag[(0, *at)] = high
        bdiag[(1, *at)] = low
    for p in range(4):
        base[p] = dot(onehot[p], bdiag[0]) + dot(onehot[p], bdiag[1])

    alphas = [points_ref[i].astype(F32) * 0.125 for i in range(8)]

    lanes = pl.ds(pl.multiple_of(128 * mine, 128), 128)
    cc = {}

    def coefs(part):
        @pl.loop(0, 5)
        def _(n):
            rows = pl.ds(pl.multiple_of(80 * part + 16 * n, 16), 16)
            eg, eu, up = acce[0, rows], acce[1, rows], accu[rows]
            cg = jnp.zeros((16, 128), F32)
            cu = jnp.zeros((16, 128), F32)
            for p in range(4):
                bg, bu = base[p, rows, 0:128], base[p, rows, 128:256]
                dg, du = eg - bg, eu - bu
                for a in alphas:
                    g = bg + a * dg
                    u = bu + a * du
                    s = 0.5 * jnp.tanh(0.5 * g) + 0.5
                    gs = g * s
                    cu = cu + gs
                    cg = cg + u * (s + gs * (1.0 - s))
            cg = up * (cg * (1.0 / 32.0))
            cu = up * (cu * (1.0 / 32.0))
            half = lax.broadcasted_iota(jnp.int32, (16, 128), 1) < 64
            first = pl.ds(pl.multiple_of(16 * n, 16), 16)
            second = pl.ds(pl.multiple_of(80 + 16 * n, 16), 16)
            sendc[part, first, :] = jnp.where(half, cg, pltpu.roll(cu, 64, 1)).astype(BF)
            sendc[part, second, :] = jnp.where(half, pltpu.roll(cg, 64, 1), cu).astype(BF)

        for i in range(1, 8):
            n = 8 * part + i
            cc[part, i] = send(sendc.at[part], full.at[part, :, lanes], cs.at[n], cr.at[n], peers[i])
        full[part, :, lanes] = sendc[part]

    def product(part, hh, col, into, at):
        rows = pl.ds(pl.multiple_of(80 * hh, 16), 80)

        @pl.loop(0, 2)
        def _(n):
            w = pl.ds(pl.multiple_of(512 * col + 256 * n, 256), 256)
            into[at, :, pl.ds(pl.multiple_of(256 * n, 256), 256)] = dot(full[part, rows, :], wcat[:, w])

    d1, d2, d3 = {}, {}, {}

    def products(part):
        for i in range(1, 8):
            cc[part, i].wait_recv()
        for i, hh in enumerate((1 - h, h)):
            at = 2 * part + i
            product(part, hh, 1 - c, d1send, at)
            d1[at] = send(d1send.at[at], d1recv.at[at], d1s.at[at], d1r.at[at], mate)
            product(part, hh, c, keep, at)
        d1[2 * part].wait_recv()
        d2send[part] = (keep[2 * part] + d1recv[2 * part]).astype(BF)
        d2[part] = send(d2send.at[part], d2recv.at[part], d2s.at[part], d2r.at[part], facing)

    def scatter(part):
        d1[2 * part + 1].wait_recv()
        v = keep[2 * part + 1] + d1recv[2 * part + 1]
        d2[part].wait_recv()
        v = (v + d2recv[part].astype(F32)).astype(BF)
        v = jnp.concatenate([v[:, 128 * t : 128 * t + 128] for t in range(4)], axis=0)
        d3send[8 * part : 8 * part + 8] = dot(pack[...], v).astype(BF).reshape(8, 48, 128)
        for p in range(8 * part, 8 * part + 8):
            if p:
                d3[p] = send(d3send.at[p], d3recv.at[p], d3s.at[p], d3r.at[p], along(OFFSETS[p]))

    coefs(0)
    coefs(1)
    products(0)
    products(1)
    scatter(0)
    scatter(1)
    total = d3send[0].astype(F32)
    for p in range(1, Z):
        d3[p].wait_recv()
        total = total + d3recv[p].astype(F32)
    fin[...] = total
    last = send(fin, finr, fs, fr, mate)
    last.wait_recv()
    other = finr[...]
    first = c == 0
    parts = []
    for block in (jnp.where(first, total, other), jnp.where(first, other, total)):
        for t in range(4):
            parts.append(jnp.where(first, block[10 * t : 10 * t + 5], block[10 * t + 5 : 10 * t + 10]))
    out_ref[...] = jnp.concatenate(parts, axis=1).astype(BF)
    for cp in pending:
        cp.wait_send()


def on_device(examples, references, gate_weight, up_weight, down_weight, cotangent, pair_ref, points):
    vm = pl.BlockSpec(memory_space=pltpu.VMEM)
    hbm = pl.BlockSpec(memory_space=pltpu.HBM)
    sm = pl.BlockSpec(memory_space=pltpu.SMEM)
    dma = pltpu.SemaphoreType.DMA
    V = pltpu.VMEM
    return pl.pallas_call(
        kernel,
        out_shape=jax.ShapeDtypeStruct((5, 1024), BF),
        in_specs=[vm, vm, vm, hbm, hbm, hbm, vm, sm, vm, hbm, hbm, vm],
        out_specs=vm,
        scratch_shapes=[
            V((448, 1024), BF), V((448, 1024), BF), V((448, 1024), BF), V((4, 208, 768), BF), V((384, 320), BF),
            V((1024, 1024), BF), V((1024, 1024), BF),
            V((4, 4, 4, 48, 256), BF), V((208, 1024), BF),
            V((4, 4, 2, 160, 128), BF), V((4, 4, 2, 160, 128), BF),
            V((4, 160, 128), F32), V((4, 160, 128), F32), V((4, 160, 128), F32),
            V((4, 160, 256), BF), V((4, 160, 256), F32),
            V((128, 128), F32), V((2, 160, 128), F32), V((160, 128), F32),
            V((2, 256, 256), BF), V((2, 160, 128), BF), V((2, 160, 1024), BF),
            V((4, 80, 512), F32), V((4, 80, 512), F32), V((4, 80, 512), F32),
            V((2, 80, 512), BF), V((2, 80, 512), BF),
            V((Z, 48, 128), BF), V((Z, 48, 128), BF), V((48, 128), F32), V((48, 128), F32),
            dma((5,)), dma((Z,)), dma((Z,)), dma((4,)), dma((4,)), dma((4,)), dma((4,)), dma((4,)), dma((4,)),
            dma((16,)), dma((16,)), dma((4,)), dma((4,)), dma((16,)), dma((16,)), dma((4,)), dma((4,)),
            dma((2,)), dma((2,)), dma((Z,)), dma((Z,)), dma, dma,
        ],
        compiler_params=pltpu.CompilerParams(
            collective_id=0, has_side_effects=True, vmem_limit_bytes=60 * 1024 * 1024
        ),
        cost_estimate=pl.CostEstimate(flops=2 * 10**9, bytes_accessed=4 * 10**6, transcendentals=10**6),
    )(
        examples, references, cotangent, gate_weight.T, up_weight.T, down_weight, pair_ref.T, points,
        jnp.asarray(compact_rows(), BF), jnp.asarray(chunk_rows(), BF),
        jnp.asarray(pack_rows(), BF), jnp.asarray(row_table()),
    )


def solution(mesh):
    split = Mesh(mesh.devices.reshape(2, Z, 2, 4, 2), ("h", "z", "c", "x", "l"))
    wide, narrow = ("h", "z", "c"), ("x", "l")
    return jax.shard_map(
        on_device,
        mesh=split,
        in_specs=(
            P(wide, narrow), P(wide, narrow), P(narrow, wide), P(narrow, wide),
            P(wide, narrow), P(wide, narrow), P(), P(),
        ),
        out_specs=P(wide, narrow),
        check_vma=False,
    )
```

time: 101 us -> 91.4 us (0.905)
  local copies, waits for them, and re-layouts: 6.26 us -> 1.32 us
  Pallas kernels: 93.9 us -> 89.8 us
    unnamed x22 -> x1, local copies, waits for them, and re-layouts: 6.26 us -> 1.32 us
    pallas_call x1, Pallas kernels: 93.9 us -> 89.8 us  [on_device(): pl.pallas_call(kernel, out_shape=jax.ShapeDtypeStruct((5, 1024), BF), in_...]
where the time goes in v2:
time: 91.4 us; the launch traced here: 91.2 us
  Pallas kernels  89.8 us (98%)
  local copies, waits for them, and re-layouts  1.32 us (1%)
    pallas_call x1, Pallas kernels, on_device(): pl.pallas_call(kernel, out_shape=jax.ShapeDtypeStruct((5, 1024), BF), in_...  89.8 us

profile of v2, /device:TPU:1, one launch (start us, length us, event | category | flops | bytes accessed | tf_op | source)
XLA Modules:
  0.0 91.2 jit_solution(10527647416007255522)
XLA Ops:
  0.0 89.8 %shard_map.118 = bf16[5,1024]{1,0:T(8,128)(2,1)} custom-call(bf16[5,1024]{1,0:T(8,128)(2,1)} %ex_ref.1, bf16[2,1024]{1,0:T(2,128)(2,1)} %rf_ref.1, bf16[5,1024]{1,0:T(8,128)(2,1)} %ct_ref.1, bf16[448,1024]{1,0:T(8,128)(2,1)} %bitcast.3, bf16[448,1024]{1,0:T(8,128)(2,1)} %bitcast.4, bf16[448,1024]{1,0:T(8,128)(2,1)} %wd_hbm.1, s32[4,320]{1,0:T(4,128)} %bitcast.5, ...), custom_call_target="tpu_custom_call" | custom-call | flops 2000000000 | bytes 4000000 | tf_op jit(solution)/shard_map/pallas_call | solution.py:377
  89.8 1.3 %copy.14 = bf16[5,1024]{1,0:T(8,128)(2,1)} copy(bf16[5,1024]{1,0:T(8,128)(2,1)} %shard_map.118) | data formatting | bytes 20480

commit v3 on v2

v3 whole, which is shorter than its diff:
```python
import functools

import jax
import jax.numpy as jnp
import numpy as np
from jax import lax
from jax.experimental import pallas as pl
from jax.experimental.pallas import tpu as pltpu
from jax.sharding import Mesh
from jax.sharding import PartitionSpec as P

MESH = pl.DeviceIdType.MESH
BF = jnp.bfloat16
F32 = jnp.float32
Z = 16
NT = (((1,), (1,)), ((), ()))


def dot(a, b):
    return jnp.dot(a, b, preferred_element_type=F32)


def dot_nt(a, b):
    return lax.dot_general(a, b, NT, preferred_element_type=F32)


OFFSETS = (0, 1, -1, 2, -2, 4, -4, 8, 3, -3, 5, -5, 6, -6, 7, -7)


def slot_of(offset):
    return next(p for p in range(Z) if (OFFSETS[p] - offset) % Z == 0)


def compact_rows():
    s = np.zeros((96, 128), np.float32)
    for t in range(8):
        for r in range(10):
            s[10 * t + r, 16 * t + r] = 1
        for i in range(2):
            s[80 + 2 * t + i, 16 * t + 10 + i] = 1
    return s


def part_rows():
    s = np.zeros((640, 640), np.float32)
    for t in range(8):
        for q in range(8):
            for i in range(5):
                s[80 * t + 5 * q + i, 80 * q + 10 * t + i] = 1
                s[80 * t + 40 + 5 * q + i, 80 * q + 10 * t + 5 + i] = 1
    return s


def reference_rows():
    s = np.zeros((256, 256), np.float32)
    for t in range(8):
        for q in range(Z):
            for i in range(2):
                s[32 * t + 2 * q + i, 16 * q + 2 * t + i] = 1
    return s


def pack_rows():
    s = np.zeros((384, 320), np.float32)
    for p in range(8):
        for t in range(4):
            for i in range(10):
                s[p * 48 + 10 * t + i, 80 * t + 40 * (i // 5) + 5 * p + i % 5] = 1
    return s


def row_table():
    t = np.zeros((160, 128), np.int32)
    for r in range(160):
        t[r, 0] = OFFSETS[8 * (r // 80) + r % 40 // 5]
        t[r, 1] = 5 * (r % 80 // 40) + r % 5
    return t


def kernel(
    ex_ref, rf_ref, ct_ref, wg_hbm, wu_hbm, wd_hbm, pair_ref, points_ref,
    sel0_ref, perm_hbm, rperm_hbm, pack_hbm, table_ref,
    out_ref,
    wg, wu, wd, perm, rperm, pack, wcat, wd2, xbuf, rbuf, xs, xr, sendb, recvb, sendr, recvr, onehot, base, acce, accu,
    bdiag, sendc, full, d1send, d1recv, keep, d2send, d2recv, d3send, d3recv, fin, finr,
    wsem, zs, zr, ws, wr, ys, yr, hs, hr, ms, mr, gs, gr, bs, br, cs, cr, d1s, d1r, d2s, d2r, d3s, d3r, fs, fr,
):
    h, z, c = lax.axis_index("h"), lax.axis_index("z"), lax.axis_index("c")
    x, l = lax.axis_index("x"), lax.axis_index("l")
    mine = 2 * x + l
    m, mh = 2 * h + c, 2 * (1 - h) + c
    pending = []

    def send(src, dst, ssem, rsem, dev):
        cp = pltpu.make_async_remote_copy(
            src_ref=src, dst_ref=dst, send_sem=ssem, recv_sem=rsem, device_id=dev, device_id_type=MESH
        )
        cp.start()
        pending.append(cp)
        return cp

    def along(offset):
        return {"z": lax.rem(z + offset + Z, Z)}

    facing, mate = {"h": 1 - h}, {"c": 1 - c}
    peers = [{"x": lax.rem(x + i // 2, 4), "l": lax.rem(l + i % 2, 2)} for i in range(8)]
    barrier = pltpu.get_barrier_semaphore()
    for dev in [along(e) for e in (8, 4, -4, 2, -2, 1, -1)] + [facing] + peers[1:] + [mate]:
        pl.semaphore_signal(barrier, inc=1, device_id=dev, device_id_type=MESH)

    loads = [
        pltpu.make_async_copy(a, b, wsem.at[i])
        for i, (a, b) in enumerate(((wg_hbm, wg), (wu_hbm, wu), (wd_hbm, wd), (perm_hbm, perm), (rperm_hbm, rperm), (pack_hbm, pack)))
    ]
    for cp in loads:
        cp.start()

    t = jnp.concatenate(
        [ex_ref[...].astype(F32), ct_ref[...].astype(F32), rf_ref[...].astype(F32), jnp.zeros((4, 1024), F32)], axis=0
    ).astype(BF)
    t = jnp.concatenate([t[:, 128 * i : 128 * i + 128] for i in range(8)], axis=0)
    t = dot(sel0_ref[...], t).astype(BF)
    xbuf[0, m, 0] = t[:80]
    rbuf[m, 0] = t[80:]
    pl.semaphore_wait(barrier, 16)

    def block(p, who):
        return xbuf.at[p // 8, who, p % 8]

    zc, wc, yc = {}, {}, {}

    def zsend(offset, e):
        p = slot_of(offset - e)
        zc[p] = send(block(slot_of(offset), m), block(p, m), zs.at[p], zr.at[p], along(e))

    def ysend(offset, e):
        p = slot_of(offset - e)
        yc[p] = send(block(slot_of(offset), mh), block(p, mh), ys.at[p], yr.at[p], along(e))

    def wsend(offset, e):
        p = slot_of(offset - e)
        wc[p] = send(rbuf.at[m, slot_of(offset)], rbuf.at[m, p], ws.at[p], wr.at[p], along(e))

    for e in (8, 4, -4, 2, -2, 1, -1):
        wsend(0, e)
    for e in (8, 4, -4):
        zsend(0, e)

    for cp in loads:
        cp.wait()

    def prep(a):
        w0 = (0, 0, 128, 256)[a]
        kk = min(256, 448 - w0)
        k = lax.broadcasted_iota(jnp.int32, (256, kk), 1) + w0
        n = lax.broadcasted_iota(jnp.int32, (256, kk), 0)
        r = n & 127
        first = 56 * (2 * a + (n >> 7))
        gate = (r < 56) & (k == first + r)
        up = (r >= 64) & (r < 120) & (k == first + r - 64)
        sg = jnp.where(gate, 1.0, 0.0).astype(BF)
        su = jnp.where(up, 1.0, 0.0).astype(BF)
        sd = jnp.where(gate | up, 1.0, 0.0).astype(BF)
        for b in range(4):
            cols = pl.ds(256 * b, 256)
            rows = pl.ds(w0, kk)
            wcat[pl.ds(256 * a, 256), cols] = (dot(sg, wg[rows, cols]) + dot(su, wu[rows, cols])).astype(BF)
            wd2[pl.ds(256 * a, 256), cols] = dot(sd, wd[rows, cols]).astype(BF)

    hc, mc, gc = {}, {}, {}

    groups = ((0, 1), (1, 5), (5, 8), (8, 12), (12, 16), (0, 8), (8, 16))

    def group(k, who):
        first, last = groups[k]
        if k > 4:
            return rbuf.at[who, pl.ds(first, last - first)]
        return xbuf.at[first // 8, who, pl.ds(first % 8, last - first)]

    def spread(k):
        for p in range(*groups[k]):
            if p not in (0, 5, 6, 7):
                (wc if k > 4 else zc)[p].wait_recv()
        at = group(k, m)
        if k not in (3, 4):
            hc[k] = send(at, at, hs.at[k], hr.at[k], facing)
        mc[k] = send(at, at, ms.at[k], mr.at[k], mate)

    def onward(k):
        if k in (3, 4):
            for p in range(*groups[k]):
                yc[p].wait_recv()
        else:
            hc[k].wait_recv()
        at = group(k, mh)
        gc[k] = send(at, at, gs.at[k], gr.at[k], mate)

    def to_owners(src, dst, at):
        for i in (7, 5, 3, 4, 1, 6, 2):
            n = 8 * at + i
            to = src.at[lax.rem(x + i // 2, 4), lax.rem(l + i % 2, 2)]
            bc[at, i] = send(to, dst.at[i], bs.at[n], br.at[n], peers[i])

    def reference_work():
        for g in (5, 6):
            mc[g].wait_recv()
            gc[g].wait_recv()
        for i in range(4):
            o = dot(rperm[...], rbuf[i].reshape(256, 128)).astype(BF)
            for t in range(8):
                xr[32 * i : 32 * i + 32, 128 * t : 128 * t + 128] = o[32 * t : 32 * t + 32]

        @pl.loop(0, 4)
        def _(n):
            cols = pl.ds(pl.multiple_of(256 * n, 256), 256)
            p = dot_nt(xr[...], wcat[cols, :]).astype(BF)
            for e in range(2):
                sendr[n, e] = p[:, 128 * e : 128 * e + 128]

        to_owners(sendr, recvr, 2)

    def work(k):
        for g in ((0, 1, 2), (3, 4))[k]:
            mc[g].wait_recv()
            gc[g].wait_recv()
        for i in range(2):
            o = [dot(perm[...], xbuf[k, 2 * i + j].reshape(640, 128)) for j in range(2)]
            for t in range(8):
                for b in range(2):
                    rows = slice(80 * t + 40 * b, 80 * t + 40 * b + 40)
                    at = slice(160 * b + 80 * i, 160 * b + 80 * i + 80)
                    xs[at, 128 * t : 128 * t + 128] = jnp.concatenate([o[0][rows], o[1][rows]], axis=0).astype(BF)
        left = lax.broadcasted_iota(jnp.int32, (80, 256), 1) & 127

        @pl.loop(0, 4)
        def _(n):
            cols = pl.ds(pl.multiple_of(256 * n, 256), 256)
            p = dot_nt(xs[0:160], wcat[cols, :]).astype(BF)
            d = dot_nt(xs[160:320], wd2[cols, :])
            d = jnp.where(left < 64, d[:80], d[80:]).astype(BF)
            for e in range(2):
                sendb[k, n, e, 0:160] = p[:, 128 * e : 128 * e + 128]
                sendb[k, n, e, 160:240] = d[:, 128 * e : 128 * e + 128]

        to_owners(sendb.at[k], recvb.at[k], k)

    bc = {}

    def owner_sum(k):
        total = sendb[k, x, l].astype(F32)
        for i in range(1, 8):
            bc[k, i].wait_recv()
            total = total + recvb[k, i].astype(F32)
        e0, e1 = total[0:80], total[80:160]
        half = lax.broadcasted_iota(jnp.int32, (80, 128), 1) < 64
        acce[0, 80 * k : 80 * k + 80] = jnp.where(half, e0, pltpu.roll(e1, 64, 1))
        acce[1, 80 * k : 80 * k + 80] = jnp.where(half, pltpu.roll(e0, 64, 1), e1)
        accu[80 * k : 80 * k + 80] = total[160:240]

    def choose():
        off, place = table_ref[:, 0:1], table_ref[:, 1:2]
        want = ((z + off + Z) & (Z - 1)) * 10 + place
        turn = jnp.where(lax.broadcasted_iota(jnp.int32, (160, 160), 1) == want, 1.0, 0.0).astype(BF)
        for hh in range(2):
            picks = pair_ref[...].astype(F32)[:, 160 * hh : 160 * hh + 160].astype(BF)
            r = dot_nt(turn, picks).astype(jnp.int32)
            delta = (((r >> 2) & 15) - z + Z) & (Z - 1)
            slot = jnp.zeros_like(delta)
            for p in range(1, Z):
                slot = jnp.where(delta == OFFSETS[p] % Z, p, slot)
            pos = (r >> 6) * 64 + ((r >> 1) & 1) * 32 + slot * 2 + (r & 1)
            lane = lax.broadcasted_iota(jnp.int32, (160, 128), 1)
            for p in range(4):
                onehot[p, :, 128 * hh : 128 * hh + 128] = jnp.where(lane == pos[:, p : p + 1], 1.0, 0.0).astype(BF)

    spread(0)
    for i in range(4):
        prep(i)
    for e in (2, -2, 1, -1):
        zsend(0, e)
    def near(far, to):
        for offset, e in {
            7: ((8, 1), (8, -1)), 5: ((4, -2), (4, 1), (4, -1)), 6: ((-4, 2), (-4, 1), (-4, -1))
        }[far]:
            to(offset, e)

    for got, to in ((wc, wsend), (zc, zsend)):
        for p in (7, 5, 6):
            got[p].wait_recv()
            near(p, to)
    spread(2)
    spread(5)
    choose()
    onward(2)
    for p in (7, 5, 6):
        near(p, ysend)
    spread(1)
    spread(6)
    onward(0)
    onward(5)
    onward(6)
    reference_work()
    onward(1)
    spread(3)
    spread(4)
    work(0)
    onward(3)
    onward(4)
    work(1)

    def bases():
        refs = sendr[x, l].astype(F32)
        for i in range(1, 8):
            bc[2, i].wait_recv()
            refs = refs + recvr[i].astype(F32)
        turned = pltpu.roll(refs, 64, 1)
        left = lax.broadcasted_iota(jnp.int32, (128, 128), 1) < 64
        diag = (
            jnp.where(left, refs, 0.0), jnp.where(left, 0.0, turned),
            jnp.where(left, turned, 0.0), jnp.where(left, 0.0, refs),
        )
        for n, block in enumerate(diag):
            high = block.astype(BF)
            low = (block - high.astype(F32)).astype(BF)
            at = (slice(128 * (n % 2), 128 * (n % 2) + 128), slice(128 * (n // 2), 128 * (n // 2) + 128))
            bdiag[(0, *at)] = high
            bdiag[(1, *at)] = low
        for p in range(4):
            base[p] = dot(onehot[p], bdiag[0]) + dot(onehot[p], bdiag[1])

    bases()
    owner_sum(0)

    alphas = [points_ref[i].astype(F32) * 0.125 for i in range(8)]

    lanes = pl.ds(pl.multiple_of(128 * mine, 128), 128)
    cc = {}

    def coefs(part):
        @pl.loop(0, 5)
        def _(n):
            rows = pl.ds(pl.multiple_of(80 * part + 16 * n, 16), 16)
            eg, eu, up = acce[0, rows], acce[1, rows], accu[rows]
            cg = jnp.zeros((16, 128), F32)
            cu = jnp.zeros((16, 128), F32)
            for p in range(4):
                bg, bu = base[p, rows, 0:128], base[p, rows, 128:256]
                dg, du = eg - bg, eu - bu
                for a in alphas:
                    g = bg + a * dg
                    u = bu + a * du
                    s = 0.5 * jnp.tanh(0.5 * g) + 0.5
                    gs = g * s
                    cu = cu + gs
                    cg = cg + u * (s + gs * (1.0 - s))
            cg = up * (cg * (1.0 / 32.0))
            cu = up * (cu * (1.0 / 32.0))
            half = lax.broadcasted_iota(jnp.int32, (16, 128), 1) < 64
            first = pl.ds(pl.multiple_of(16 * n, 16), 16)
            second = pl.ds(pl.multiple_of(80 + 16 * n, 16), 16)
            sendc[part, first, :] = jnp.where(half, cg, pltpu.roll(cu, 64, 1)).astype(BF)
            sendc[part, second, :] = jnp.where(half, pltpu.roll(cg, 64, 1), cu).astype(BF)

        for i in range(1, 8):
            n = 8 * part + i
            cc[part, i] = send(sendc.at[part], full.at[part, :, lanes], cs.at[n], cr.at[n], peers[i])
        full[part, :, lanes] = sendc[part]

    def product(part, hh, col, into, at):
        rows = pl.ds(pl.multiple_of(80 * hh, 16), 80)

        @pl.loop(0, 2)
        def _(n):
            w = pl.ds(pl.multiple_of(512 * col + 256 * n, 256), 256)
            into[at, :, pl.ds(pl.multiple_of(256 * n, 256), 256)] = dot(full[part, rows, :], wcat[:, w])

    d1, d2, d3 = {}, {}, {}

    def products(part):
        for i in range(1, 8):
            cc[part, i].wait_recv()
        for i, hh in enumerate((1 - h, h)):
            at = 2 * part + i
            product(part, hh, 1 - c, d1send, at)
            d1[at] = send(d1send.at[at], d1recv.at[at], d1s.at[at], d1r.at[at], mate)
            product(part, hh, c, keep, at)

    def face(part):
        d1[2 * part].wait_recv()
        d2send[part] = (keep[2 * part] + d1recv[2 * part]).astype(BF)
        d2[part] = send(d2send.at[part], d2recv.at[part], d2s.at[part], d2r.at[part], facing)

    def scatter(part):
        d1[2 * part + 1].wait_recv()
        v = keep[2 * part + 1] + d1recv[2 * part + 1]
        d2[part].wait_recv()
        v = (v + d2recv[part].astype(F32)).astype(BF)
        v = jnp.concatenate([v[:, 128 * t : 128 * t + 128] for t in range(4)], axis=0)
        d3send[8 * part : 8 * part + 8] = dot(pack[...], v).astype(BF).reshape(8, 48, 128)
        for p in range(8 * part, 8 * part + 8):
            if p:
                d3[p] = send(d3send.at[p], d3recv.at[p], d3s.at[p], d3r.at[p], along(OFFSETS[p]))

    coefs(0)
    owner_sum(1)
    coefs(1)
    for part in range(2):
        products(part)
        face(part)
    scatter(0)
    scatter(1)
    total = d3send[0].astype(F32)
    for p in range(1, Z):
        d3[p].wait_recv()
        total = total + d3recv[p].astype(F32)
    fin[...] = total
    last = send(fin, finr, fs, fr, mate)
    last.wait_recv()
    other = finr[...]
    first = c == 0
    parts = []
    for block in (jnp.where(first, total, other), jnp.where(first, other, total)):
        for t in range(4):
            parts.append(jnp.where(first, block[10 * t : 10 * t + 5], block[10 * t + 5 : 10 * t + 10]))
    out_ref[...] = jnp.concatenate(parts, axis=1).astype(BF)
    for cp in pending:
        cp.wait_send()


def on_device(examples, references, gate_weight, up_weight, down_weight, cotangent, pair_ref, points):
    vm = pl.BlockSpec(memory_space=pltpu.VMEM)
    hbm = pl.BlockSpec(memory_space=pltpu.HBM)
    sm = pl.BlockSpec(memory_space=pltpu.SMEM)
    dma = pltpu.SemaphoreType.DMA
    V = pltpu.VMEM
    return pl.pallas_call(
        kernel,
        out_shape=jax.ShapeDtypeStruct((5, 1024), BF),
        in_specs=[vm, vm, vm, hbm, hbm, hbm, vm, sm, vm, hbm, hbm, hbm, vm],
        out_specs=vm,
        scratch_shapes=[
            V((448, 1024), BF), V((448, 1024), BF), V((448, 1024), BF),
            V((640, 640), BF), V((256, 256), BF), V((384, 320), BF),
            V((1024, 1024), BF), V((1024, 1024), BF),
            V((2, 4, 8, 80, 128), BF), V((4, Z, 16, 128), BF), V((320, 1024), BF), V((128, 1024), BF),
            V((2, 4, 2, 240, 128), BF), V((2, 8, 240, 128), BF),
            V((4, 2, 128, 128), BF), V((8, 128, 128), BF),
            V((4, 160, 256), BF), V((4, 160, 256), F32),
            V((2, 160, 128), F32), V((160, 128), F32),
            V((2, 256, 256), BF), V((2, 160, 128), BF), V((2, 160, 1024), BF),
            V((4, 80, 512), F32), V((4, 80, 512), F32), V((4, 80, 512), F32),
            V((2, 80, 512), BF), V((2, 80, 512), BF),
            V((Z, 48, 128), BF), V((Z, 48, 128), BF), V((48, 128), F32), V((48, 128), F32),
            dma((6,)), dma((Z,)), dma((Z,)), dma((Z,)), dma((Z,)), dma((Z,)), dma((Z,)), dma((7,)), dma((7,)), dma((7,)), dma((7,)),
            dma((7,)), dma((7,)), dma((24,)), dma((24,)), dma((16,)), dma((16,)), dma((4,)), dma((4,)),
            dma((2,)), dma((2,)), dma((Z,)), dma((Z,)), dma, dma,
        ],
        compiler_params=pltpu.CompilerParams(
            collective_id=0, has_side_effects=True, vmem_limit_bytes=60 * 1024 * 1024
        ),
        cost_estimate=pl.CostEstimate(flops=2 * 10**9, bytes_accessed=4 * 10**6, transcendentals=10**6),
    )(
        examples, references, cotangent, gate_weight.T, up_weight.T, down_weight, pair_ref.T, points,
        jnp.asarray(compact_rows(), BF), jnp.asarray(part_rows(), BF), jnp.asarray(reference_rows(), BF),
        jnp.asarray(pack_rows(), BF), jnp.asarray(row_table()),
    )


def solution(mesh):
    split = Mesh(mesh.devices.reshape(2, Z, 2, 4, 2), ("h", "z", "c", "x", "l"))
    wide, narrow = ("h", "z", "c"), ("x", "l")
    return jax.shard_map(
        on_device,
        mesh=split,
        in_specs=(
            P(wide, narrow), P(wide, narrow), P(narrow, wide), P(narrow, wide),
            P(wide, narrow), P(wide, narrow), P(), P(),
        ),
        out_specs=P(wide, narrow),
        check_vma=False,
    )
```

time: 91.4 us -> 87.3 us (0.955)
  Pallas kernels: 89.8 us -> 85.7 us
    pallas_call x1, Pallas kernels: 89.8 us -> 85.7 us  [on_device(): pl.pallas_call(kernel, out_shape=jax.ShapeDtypeStruct((5, 1024), BF), in_...]
where the time goes in v3:
time: 87.3 us; the launch traced here: 87.1 us
  Pallas kernels  85.7 us (98%)
  local copies, waits for them, and re-layouts  1.32 us (2%)
    pallas_call x1, Pallas kernels, on_device(): pl.pallas_call(kernel, out_shape=jax.ShapeDtypeStruct((5, 1024), BF), in_...  85.7 us

profile of v3, /device:TPU:1, one launch (start us, length us, event | category | flops | bytes accessed | tf_op | source)
XLA Modules:
  0.0 87.1 jit_solution(17352411500283580819)
XLA Ops:
  0.0 85.7 %shard_map.127 = bf16[5,1024]{1,0:T(8,128)(2,1)} custom-call(bf16[5,1024]{1,0:T(8,128)(2,1)} %ex_ref.1, bf16[2,1024]{1,0:T(2,128)(2,1)} %rf_ref.1, bf16[5,1024]{1,0:T(8,128)(2,1)} %ct_ref.1, bf16[448,1024]{1,0:T(8,128)(2,1)} %bitcast.3, bf16[448,1024]{1,0:T(8,128)(2,1)} %bitcast.4, bf16[448,1024]{1,0:T(8,128)(2,1)} %wd_hbm.1, s32[4,320]{1,0:T(4,128)} %bitcast.5, ...), custom_call_target="tpu_custom_call" | custom-call | flops 2000000000 | bytes 4000000 | tf_op jit(solution)/shard_map/pallas_call | solution.py:436
  85.8 1.3 %copy.15 = bf16[5,1024]{1,0:T(8,128)(2,1)} copy(bf16[5,1024]{1,0:T(8,128)(2,1)} %shard_map.127) | data formatting | bytes 20480

commit v4 on v3

--- a/solution.py
+++ b/solution.py
@@ -361,9 +361,13 @@
             sendc[part, first, :] = jnp.where(half, cg, pltpu.roll(cu, 64, 1)).astype(BF)
             sendc[part, second, :] = jnp.where(half, pltpu.roll(cg, 64, 1), cu).astype(BF)
 
-        for i in range(1, 8):
-            n = 8 * part + i
-            cc[part, i] = send(sendc.at[part], full.at[part, :, lanes], cs.at[n], cr.at[n], peers[i])
+        for b, hh in enumerate((1 - h, h)):
+            rows = pl.ds(pl.multiple_of(80 * hh, 16), 80)
+            for i in range(1, 8):
+                n = 16 * part + 8 * b + i
+                cc[part, b, i] = send(
+                    sendc.at[part, rows], full.at[part, rows, lanes], cs.at[n], cr.at[n], peers[i]
+                )
         full[part, :, lanes] = sendc[part]
 
     def product(part, hh, col, into, at):
@@ -378,17 +382,22 @@
 
     def products(part):
         for i in range(1, 8):
-            cc[part, i].wait_recv()
-        for i, hh in enumerate((1 - h, h)):
-            at = 2 * part + i
-            product(part, hh, 1 - c, d1send, at)
-            d1[at] = send(d1send.at[at], d1recv.at[at], d1s.at[at], d1r.at[at], mate)
-            product(part, hh, c, keep, at)
-
-    def face(part):
-        d1[2 * part].wait_recv()
-        d2send[part] = (keep[2 * part] + d1recv[2 * part]).astype(BF)
+            cc[part, 0, i].wait_recv()
+        at = 2 * part
+
+        def lend(i, hh):
+            product(part, hh, 1 - c, d1send, at + i)
+            d1[at + i] = send(d1send.at[at + i], d1recv.at[at + i], d1s.at[at + i], d1r.at[at + i], mate)
+
+        lend(0, 1 - h)
+        product(part, 1 - h, c, keep, at)
+        d1[at].wait_recv()
+        d2send[part] = (keep[at] + d1recv[at]).astype(BF)
         d2[part] = send(d2send.at[part], d2recv.at[part], d2s.at[part], d2r.at[part], facing)
+        for i in range(1, 8):
+            cc[part, 1, i].wait_recv()
+        lend(1, h)
+        product(part, h, c, keep, at + 1)
 
     def scatter(part):
         d1[2 * part + 1].wait_recv()
@@ -404,9 +413,8 @@
     coefs(0)
     owner_sum(1)
     coefs(1)
-    for part in range(2):
-        products(part)
-        face(part)
+    products(0)
+    products(1)
     scatter(0)
     scatter(1)
     total = d3send[0].astype(F32)
@@ -452,7 +460,7 @@
             V((2, 80, 512), BF), V((2, 80, 512), BF),
             V((Z, 48, 128), BF), V((Z, 48, 128), BF), V((48, 128), F32), V((48, 128), F32),
             dma((6,)), dma((Z,)), dma((Z,)), dma((Z,)), dma((Z,)), dma((Z,)), dma((Z,)), dma((7,)), dma((7,)), dma((7,)), dma((7,)),
-            dma((7,)), dma((7,)), dma((24,)), dma((24,)), dma((16,)), dma((16,)), dma((4,)), dma((4,)),
+            dma((7,)), dma((7,)), dma((24,)), dma((24,)), dma((32,)), dma((32,)), dma((4,)), dma((4,)),
             dma((2,)), dma((2,)), dma((Z,)), dma((Z,)), dma, dma,
         ],
         compiler_params=pltpu.CompilerParams(

time: 87.3 us -> 86.9 us (level)
  no operation moved by 1% of the time
where the time goes in v4:
time: 86.9 us; the launch traced here: 86.7 us
  Pallas kernels  85.3 us (98%)
  local copies, waits for them, and re-layouts  1.32 us (2%)
    pallas_call x1, Pallas kernels, on_device(): pl.pallas_call(kernel, out_shape=jax.ShapeDtypeStruct((5, 1024), BF), in_...  85.3 us

profile of v4, /device:TPU:1, one launch (start us, length us, event | category | flops | bytes accessed | tf_op | source)
XLA Modules:
  0.0 86.7 jit_solution(4624362821739245610)
XLA Ops:
  0.0 85.3 %shard_map.127 = bf16[5,1024]{1,0:T(8,128)(2,1)} custom-call(bf16[5,1024]{1,0:T(8,128)(2,1)} %ex_ref.1, bf16[2,1024]{1,0:T(2,128)(2,1)} %rf_ref.1, bf16[5,1024]{1,0:T(8,128)(2,1)} %ct_ref.1, bf16[448,1024]{1,0:T(8,128)(2,1)} %bitcast.3, bf16[448,1024]{1,0:T(8,128)(2,1)} %bitcast.4, bf16[448,1024]{1,0:T(8,128)(2,1)} %wd_hbm.1, s32[4,320]{1,0:T(4,128)} %bitcast.5, ...), custom_call_target="tpu_custom_call" | custom-call | flops 2000000000 | bytes 4000000 | tf_op jit(solution)/shard_map/pallas_call | solution.py:444
  85.4 1.3 %copy.15 = bf16[5,1024]{1,0:T(8,128)(2,1)} copy(bf16[5,1024]{1,0:T(8,128)(2,1)} %shard_map.127) | data formatting | bytes 20480

commit v5 on v4

--- a/solution.py
+++ b/solution.py
@@ -414,8 +414,8 @@
     owner_sum(1)
     coefs(1)
     products(0)
+    scatter(0)
     products(1)
-    scatter(0)
     scatter(1)
     total = d3send[0].astype(F32)
     for p in range(1, Z):

time: 86.9 us -> 88.7 us (1.021)
  Pallas kernels: 85.3 us -> 87.2 us
    pallas_call x1, Pallas kernels: 85.3 us -> 87.2 us  [on_device(): pl.pallas_call(kernel, out_shape=jax.ShapeDtypeStruct((5, 1024), BF), in_...]
where the time goes in v5:
time: 88.7 us; the launch traced here: 88.5 us
  Pallas kernels  87.2 us (98%)
  local copies, waits for them, and re-layouts  1.32 us (1%)
    pallas_call x1, Pallas kernels, on_device(): pl.pallas_call(kernel, out_shape=jax.ShapeDtypeStruct((5, 1024), BF), in_...  87.2 us

profile of v5, /device:TPU:1, one launch (start us, length us, event | category | flops | bytes accessed | tf_op | source)
XLA Modules:
  0.0 88.5 jit_solution(6257627959885649643)
XLA Ops:
  0.0 87.2 %shard_map.127 = bf16[5,1024]{1,0:T(8,128)(2,1)} custom-call(bf16[5,1024]{1,0:T(8,128)(2,1)} %ex_ref.1, bf16[2,1024]{1,0:T(2,128)(2,1)} %rf_ref.1, bf16[5,1024]{1,0:T(8,128)(2,1)} %ct_ref.1, bf16[448,1024]{1,0:T(8,128)(2,1)} %bitcast.3, bf16[448,1024]{1,0:T(8,128)(2,1)} %bitcast.4, bf16[448,1024]{1,0:T(8,128)(2,1)} %wd_hbm.1, s32[4,320]{1,0:T(4,128)} %bitcast.5, ...), custom_call_target="tpu_custom_call" | custom-call | flops 2000000000 | bytes 4000000 | tf_op jit(solution)/shard_map/pallas_call | solution.py:444
  87.2 1.3 %copy.15 = bf16[5,1024]{1,0:T(8,128)(2,1)} copy(bf16[5,1024]{1,0:T(8,128)(2,1)} %shard_map.127) | data formatting | bytes 20480
